TPU v7x, 32 devices: a whole 2x2x4 slice. The times are simulated.
32 devices in a mesh: groups: 2 (over x), view: 16 (over z, y, core).
Axes of the slice: x: 2, y: 2, z: 4, core: 2. Of those that a mesh axis runs over, the one named last changes fastest.
Arguments:
- estimate: float32 [6144, 128], P(('groups', 'view')), parts along dimension 0, may hold values from 0.5 to 2, as said below
- measured: bfloat16 [512, 192, 128], P(('groups', 'view')), parts along dimension 0, may hold values from 0.25 to 4, as said below
- kernel_z: bfloat16 [16, 3, 128, 128], replicated, may hold values from 0 to 2, as said below
- kernel_x: bfloat16 [16, 3, 12, 12], replicated, may hold values from 0 to 2, as said below
- kernel_y: bfloat16 [16, 3, 16, 16], replicated, may hold values from 0 to 2, as said below
- background: bfloat16 [16], replicated, may hold values from 0.049804688 to 0.5
- relax: bfloat16 [16], replicated, may hold values from 0.029907227 to 0.23925781
- owner: int32 [512, 1], P(('groups', 'view')), parts along dimension 0, may hold values from 0 to 15; in each aligned block of 16 rows (0 to 15, 16 to 31, ...) at most 2 rows name the same one
- source_offset: int32 [512], P(('groups', 'view')), parts along dimension 0, may hold values from 0 to 184
- tile_offset: int32 [512], P(('groups', 'view')), parts along dimension 0, may hold values from 0 to 56
- feather: int32 [512, 8], P(('groups', 'view')), parts along dimension 0, may hold values from 1 to 8
Outputs:
- refined: float32 [6144, 128], P(('groups', 'view')), parts along dimension 0
- smoothed: float32 [2048, 128], P(('groups', 'view')), parts along dimension 0
There are 2 independent parts, one for each index of `groups`. A program takes and returns all parts, laid end to end along the dimension named above; an argument that names none is the same for every part. Nothing has to cross between parts.
Inputs may be any that keep to these rules, and one draw needn't show every extreme that they name: `owner`: within the 16 rows of one block no tile is named more than 2 times, and in every draw some tile is named exactly 2 times by some block. `kernel_z`: entries are nonnegative and every diagonal entry is positive. `kernel_x`: entries are nonnegative and every diagonal entry is positive. `kernel_y`: entries are nonnegative and every diagonal entry is positive. `estimate`: entries are positive. `measured`: entries are positive.
All inputs are finite; a program needn't handle non-finite values.
Results may differ from a plain program's by a relative error of at most 0.0006.
Values may be sent and summed in bfloat16 or wider, within the bound.
No kernel may reach another device: no remote copies, remote signals or barrier semaphores. Data moves between devices by JAX's collectives and lax.ppermute only.
A program may use at most 64 MiB of HBM per device.

v0:
```python
import jax
import jax.numpy as jnp
from jax import lax
from jax.sharding import PartitionSpec as P

VIEWS = 16
SROWS = 8
TROWS = 64
CAP = 2


smooth_rate = 0.24
edge_scale = 1.0


def from_behind(block, axis, distance):
    devices = range(lax.axis_size(axis))
    route = [((i - distance) % len(devices), i) for i in devices]
    return lax.ppermute(block, axis, route)


def with_halo(block, sides, width):
    for axis, dim in sides:
        count = lax.axis_size(axis)
        forward = [(i, i + 1) for i in range(count - 1)]
        backward = [(target, source) for source, target in forward]
        low = lax.ppermute(
            lax.slice_in_dim(block, block.shape[dim] - width, None, axis=dim), axis, forward
        )
        high = lax.ppermute(lax.slice_in_dim(block, 0, width, axis=dim), axis, backward)
        block = jnp.concatenate([low, block, high], axis=dim)
    return block


def kron_rows(kernel_x, kernel_y):
    outer = (
        kernel_x.astype(jnp.float32)[..., :, None, :, None]
        * kernel_y.astype(jnp.float32)[..., None, :, None, :]
    )
    rows_xy = kernel_x.shape[-1] * kernel_y.shape[-1]
    return outer.reshape(outer.shape[:-4] + (rows_xy, rows_xy)).astype(jnp.bfloat16)


def visit_view(block, kernel_z, kernel_xy, measured_block, back_value, relax_value):
    lowered = block.astype(jnp.bfloat16)
    along_z = jnp.einsum(
        "iz,rkz->rik", lowered, kernel_z, preferred_element_type=jnp.float32
    ).astype(jnp.bfloat16)
    forward = jnp.einsum("rij,rjk->ik", kernel_xy, along_z, preferred_element_type=jnp.float32)
    ratio_lo = (measured_block.astype(jnp.float32) / (forward + back_value)).astype(jnp.bfloat16)
    back_z = jnp.einsum(
        "ik,rkz->riz", ratio_lo, kernel_z, preferred_element_type=jnp.float32
    ).astype(jnp.bfloat16)
    adjoint = jnp.einsum("rji,rjz->iz", kernel_xy, back_z, preferred_element_type=jnp.float32)
    column_xy = jnp.sum(kernel_xy.astype(jnp.float32), axis=1)
    column_z = jnp.sum(kernel_z.astype(jnp.float32), axis=1)
    weights_sum = jnp.einsum("ri,rz->iz", column_xy, column_z, precision=lax.Precision.HIGHEST)
    return block * jnp.exp(relax_value * jnp.log(adjoint / weights_sum))


def fetch_record(piece, offset):
    return from_behind(piece, "view", offset)


def on_device(
    estimate,
    measured,
    kernel_z,
    kernel_x,
    kernel_y,
    background,
    relax,
    owner,
    source_offset,
    tile_offset,
    feather,
):
    view_count = lax.axis_size("view")
    position = lax.axis_index("view")
    depth = estimate.shape[1]
    back_values = background.astype(jnp.float32)
    relax_values = relax.astype(jnp.float32)
    arrived = [measured[0]]
    for stop_id in range(1, VIEWS):
        arrived.append(fetch_record(measured[stop_id], -stop_id))
    records = jnp.stack(arrived, axis=0)

    def advance(stop_id, carried):
        view_id = (position + stop_id) % VIEWS
        kernel_xy = kron_rows(kernel_x[view_id], kernel_y[view_id])
        measured_block = lax.dynamic_index_in_dim(records, stop_id, 0, keepdims=False)
        return visit_view(
            carried,
            kernel_z[view_id],
            kernel_xy,
            measured_block,
            back_values[view_id],
            relax_values[view_id],
        )

    refined = lax.fori_loop(0, VIEWS, advance, estimate)
    listed = owner.shape[0]
    targets = owner[:, 0]
    window_rows = jnp.arange(SROWS, dtype=jnp.int32)
    sources = source_offset[:, None] + window_rows[None, :]
    weights = feather.astype(jnp.float32)
    pieces = refined[sources] * weights[..., None]
    entry_ids = jnp.arange(listed, dtype=jnp.int32)
    earlier = (targets[:, None] == targets[None, :]) & (entry_ids[None, :] < entry_ids[:, None])
    rank_in = jnp.sum(earlier.astype(jnp.int32), axis=1)
    slot_ids = targets * CAP + rank_in
    data_buf = (
        jnp.zeros((view_count * CAP, SROWS, depth), jnp.float32)
        .at[slot_ids]
        .set(pieces)
        .reshape(view_count, CAP, SROWS, depth)
    )
    weight_buf = (
        jnp.zeros((view_count * CAP, SROWS), jnp.float32)
        .at[slot_ids]
        .set(weights)
        .reshape(view_count, CAP, SROWS)
    )
    offset_buf = (
        jnp.zeros((view_count * CAP,), jnp.float32)
        .at[slot_ids]
        .set(tile_offset.astype(jnp.float32))
        .reshape(view_count, CAP)
    )
    data_in = lax.all_to_all(data_buf, "view", split_axis=0, concat_axis=0, tiled=True)
    weight_in = lax.all_to_all(weight_buf, "view", split_axis=0, concat_axis=0, tiled=True)
    offset_in = lax.all_to_all(offset_buf, "view", split_axis=0, concat_axis=0, tiled=True)
    tile_rows = jnp.arange(TROWS, dtype=jnp.float32)
    placed = (
        offset_in[:, :, None, None] + window_rows.astype(jnp.float32)[None, None, :, None]
        == tile_rows[None, None, None, :]
    ).astype(jnp.float32)
    summed = jnp.einsum("ncrt,ncrz->ctz", placed, data_in, precision=lax.Precision.HIGHEST)
    counted = jnp.einsum("ncrt,ncr->ct", placed, weight_in, precision=lax.Precision.HIGHEST)
    summed, counted = (summed, counted)
    numerator = 1.0 + jnp.sum(summed, axis=0)
    denominator = 1.0 + jnp.sum(counted, axis=0)
    joined = numerator / denominator[:, None]
    framed = with_halo(joined, (("view", 0),), 1)
    padded = jnp.pad(framed, ((0, 0), (1, 1)))
    flux_sum = jnp.zeros_like(joined)
    for neighbor in (padded[2:, 1:-1], padded[:-2, 1:-1], padded[1:-1, 2:], padded[1:-1, :-2]):
        change = neighbor - joined
        flux_sum = flux_sum + change / (1.0 + change / edge_scale * (change / edge_scale))
    smoothed = joined + smooth_rate * flux_sum
    return (refined, smoothed)


def solution(mesh):
    return jax.shard_map(
        on_device,
        mesh=mesh,
        in_specs=(
            P(("groups", "view"), None),
            P(("groups", "view"), None, None),
            P(),
            P(),
            P(),
            P(),
            P(),
            P(("groups", "view"), None),
            P(("groups", "view")),
            P(("groups", "view")),
            P(("groups", "view"), None),
        ),
        out_specs=(P(("groups", "view"), None), P(("groups", "view"), None)),
        check_vma=False,
    )
```

profile of v0, /device:TPU:0, one launch (start us, length us, event | category | flops | bytes accessed | tf_op | source)
XLA Modules:
  0.0 238.4 jit_solution(7790270060859869322)
XLA Ops:
  2.0 5.5 %collective-permute-start = (bf16[192,128]{1,0:T(8,128)(2,1)S(1)}, bf16[192,128]{1,0:T(8,128)(2,1)S(1)}, u32[]{:S(2)}, u32[]{:S(2)}) collective-permute-start(bf16[192,128]{1,0:T(8,128)(2,1)S(1)} %get-tuple-element.293), channel_id=1, source_target_pairs={{1,0},{2,1},{3,2},{4,3},{5,4},{6,5},{7,6},{8,7},{9,8},{10,9},{11,1... | collective-permute-start | bytes 147464 | tf_op jit(solution)/shard_map/ppermute | solution.py:19
  10.5 6.7 %all-to-all-start = ((f32[16,1,2]{2,1,0:T(1,128)}), f32[16,1,2]{2,1,0:T(1,128)S(1)}, u32[]{:S(2)}, u32[]{:S(2)}) async-start(f32[16,1,2]{2,1,0:T(1,128)} %bitcast.45), calls=%async_computation | async-start | bytes 16384 | tf_op jit(solution)/shard_map/all_to_all | solution.py:132
  18.8 4.7 %all-to-all-done = f32[16,1,2]{2,1,0:T(1,128)S(1)} async-done(((f32[16,1,2]{2,1,0:T(1,128)}), f32[16,1,2]{2,1,0:T(1,128)S(1)}, u32[]{:S(2)}, u32[]{:S(2)}) %all-to-all-start) | async-done | bytes 160 | tf_op jit(solution)/shard_map/all_to_all | solution.py:132
  23.5 3.5 %all-to-all-start.2 = ((f32[16,2,8]{2,1,0:T(2,128)}), f32[16,2,8]{2,1,0:T(2,128)S(1)}, u32[]{:S(2)}, u32[]{:S(2)}) async-start(f32[16,2,8]{2,1,0:T(2,128)} %bitcast.51), calls=%async_computation.2 | async-start | bytes 32768 | tf_op jit(solution)/shard_map/all_to_all | solution.py:131
  27.1 3.7 %collective-permute-start.5 = (bf16[192,128]{1,0:T(8,128)(2,1)S(1)}, bf16[192,128]{1,0:T(8,128)(2,1)S(1)}, u32[]{:S(2)}, u32[]{:S(2)}) collective-permute-start(bf16[192,128]{1,0:T(8,128)(2,1)S(1)} %get-tuple-element.288), channel_id=1, source_target_pairs={{6,0},{7,1},{8,2},{9,3},{10,4},{11,5},{12,6},{13,7},{14,8},{15,9},... | collective-permute-start | bytes 147464 | tf_op jit(solution)/shard_map/ppermute | solution.py:19
  30.9 2.4 %collective-permute-start.7 = (bf16[192,128]{1,0:T(8,128)(2,1)S(1)}, bf16[192,128]{1,0:T(8,128)(2,1)S(1)}, u32[]{:S(2)}, u32[]{:S(2)}) collective-permute-start(bf16[192,128]{1,0:T(8,128)(2,1)S(1)} %get-tuple-element.286), channel_id=1, source_target_pairs={{8,0},{9,1},{10,2},{11,3},{12,4},{13,5},{14,6},{15,7},{0,8},{1,9},... | collective-permute-start | bytes 147464 | tf_op jit(solution)/shard_map/ppermute | solution.py:19
  33.9 2.5 %collective-permute-start.9 = (bf16[192,128]{1,0:T(8,128)(2,1)S(1)}, bf16[192,128]{1,0:T(8,128)(2,1)S(1)}, u32[]{:S(2)}, u32[]{:S(2)}) collective-permute-start(bf16[192,128]{1,0:T(8,128)(2,1)S(1)} %get-tuple-element.284), channel_id=1, source_target_pairs={{10,0},{11,1},{12,2},{13,3},{14,4},{15,5},{0,6},{1,7},{2,8},{3,9},... | collective-permute-start | bytes 147464 | tf_op jit(solution)/shard_map/ppermute | solution.py:19
  37.4 1.9 collective-permute-start.11
  42.5 2.7 %collective-permute-done.9 = bf16[192,128]{1,0:T(8,128)(2,1)S(1)} collective-permute-done((bf16[192,128]{1,0:T(8,128)(2,1)S(1)}, bf16[192,128]{1,0:T(8,128)(2,1)S(1)}, u32[]{:S(2)}, u32[]{:S(2)}) %collective-permute-start.9) | collective-permute-done | bytes 49184 | tf_op jit(solution)/shard_map/ppermute | solution.py:19
  48.2 3.2 %collective-permute-done.14 = bf16[192,128]{1,0:T(8,128)(2,1)S(1)} collective-permute-done((bf16[192,128]{1,0:T(8,128)(2,1)S(1)}, bf16[192,128]{1,0:T(8,128)(2,1)S(1)}, u32[]{:S(2)}, u32[]{:S(2)}) %collective-permute-start.14) | collective-permute-done | bytes 49184 | tf_op jit(solution)/shard_map/ppermute | solution.py:19
  51.4 166.8 %while.15 = (s32[]{:T(128)}, f32[192,128]{1,0:T(8,128)S(1)}, s32[]{:T(128)}, f32[16]{0:T(128)S(1)}, bf16[16,3,12,12]{3,2,1,0:T(8,128)(2,1)S(1)}, /*index=5*/bf16...) while((s32[]{:T(128)}, f32[192,128]{1,0:T(8,128)S(1)}, ...), condition=%wide.region_3.4_spmd, body=%wide.region_0.3_spmd.sunk | while | flops 96141568 | bytes 8356960 | solution.py:101
  53.5 1.8 convert_element_type.219
  55.9 2.0 fusion.71
  63.9 1.8 convert_element_type.219
  66.3 2.0 fusion.71
  76.7 2.0 fusion.71
  87.2 2.0 fusion.71
  97.6 2.0 fusion.71
  108.0 2.0 fusion.71
  118.4 2.0 fusion.71
  128.9 2.0 fusion.71
  139.3 2.0 fusion.71
  149.7 2.0 fusion.71
  160.1 2.0 fusion.71
  170.5 2.0 fusion.71
  181.0 2.0 fusion.71
  191.4 2.0 fusion.71
  201.8 2.0 fusion.71
  212.2 2.0 fusion.71
  220.7 3.5 %all-to-all-start.1 = ((f32[16,2,8,128]{3,1,2,0:T(2,128)}), f32[16,2,8,128]{3,1,2,0:T(2,128)S(1)}, u32[]{:S(2)}, u32[]{:S(2)}) async-start(f32[16,2,8,128]{3,1,2,0:T(2,128)} %copy.36), calls=%async_computation.1 | async-start | bytes 262144 | tf_op jit(solution)/shard_map/all_to_all | solution.py:130
  224.6 7.5 %all-to-all-done.1 = f32[16,2,8,128]{3,1,2,0:T(2,128)S(1)} async-done(((f32[16,2,8,128]{3,1,2,0:T(2,128)}), f32[16,2,8,128]{3,1,2,0:T(2,128)S(1)}, u32[]{:S(2)}, u32[]{:S(2)}) %all-to-all-start.1) | async-done | bytes 131104 | tf_op jit(solution)/shard_map/all_to_all | solution.py:130
  233.7 3.0 %collective-permute-start.16 = (f32[1,128]{1,0:T(1,128)S(1)}, f32[1,128]{1,0:T(1,128)S(1)}, u32[]{:S(2)}, u32[]{:S(2)}) collective-permute-start(f32[1,128]{1,0:T(1,128)S(1)} %get-tuple-element.296), channel_id=1, source_target_pairs={{0,1},{1,2},{2,3},{3,4},{4,5},{5,6},{6,7},{7,8},{8,9},{9,10},{10,1... | collective-permute-start | bytes 1544 | tf_op jit(solution)/shard_map/ppermute | solution.py:27
  (311 shorter events, 149.8 us)
Async XLA Ops:
  0.6 16.8 %copy-start.2 = (bf16[16,3,12,12]{3,0,2,1:T(8,128)(2,1)S(1)}, bf16[16,3,12,12]{3,0,2,1:T(8,128)(2,1)}, u32[]{:S(2)}) copy-start(bf16[16,3,12,12]{3,0,2,1:T(8,128)(2,1)} %param.16) | copy-start | bytes 41476
  0.6 16.8 %copy-start.10 = (bf16[16]{0:T(256)(128)(2,1)S(1)}, bf16[16]{0:T(256)(128)(2,1)}, u32[]{:S(2)}) copy-start(bf16[16]{0:T(256)(128)(2,1)} %param.18) | copy-start | bytes 100
  0.7 16.8 %copy-start.9 = (bf16[16]{0:T(256)(128)(2,1)S(1)}, bf16[16]{0:T(256)(128)(2,1)}, u32[]{:S(2)}) copy-start(bf16[16]{0:T(256)(128)(2,1)} %param.19) | copy-start | bytes 100
  0.7 8.3 %copy-start.7 = (s32[16,1]{0,1:T(1,128)S(1)}, s32[16,1]{0,1:T(1,128)}, u32[]{:S(2)}) copy-start(s32[16,1]{0,1:T(1,128)} %param.20) | copy-start | bytes 196
  0.7 16.5 %copy-start.6 = (s32[16]{0:T(128)S(1)}, s32[16]{0:T(128)}, u32[]{:S(2)}) copy-start(s32[16]{0:T(128)} %param.21) | copy-start | bytes 196
  0.7 8.4 %copy-start.8 = (s32[16]{0:T(128)S(1)}, s32[16]{0:T(128)}, u32[]{:S(2)}) copy-start(s32[16]{0:T(128)} %param.22) | copy-start | bytes 196
  0.7 16.8 %copy-start.3 = (s32[16,8]{0,1:T(8,128)S(1)}, s32[16,8]{0,1:T(8,128)}, u32[]{:S(2)}) copy-start(s32[16,8]{0,1:T(8,128)} %param.23) | copy-start | bytes 1540
  0.7 50.7 %copy-start.1 = (f32[192,128]{1,0:T(8,128)S(1)}, f32[192,128]{1,0:T(8,128)}, u32[]{:S(2)}) copy-start(f32[192,128]{1,0:T(8,128)} %param.13) | copy-start | bytes 294916
  2.0 25.1 %collective-permute-start = (bf16[192,128]{1,0:T(8,128)(2,1)S(1)}, bf16[192,128]{1,0:T(8,128)(2,1)S(1)}, u32[]{:S(2)}, u32[]{:S(2)}) collective-permute-start(bf16[192,128]{1,0:T(8,128)(2,1)S(1)} %get-tuple-element.293), channel_id=1, source_target_pairs={{1,0},{2,1},{3,2},{4,3},{5,4},{6,5},{7,6},{8,7},{9,8},{10,9},{11,1... | collective-permute-start | bytes 147464 | tf_op jit(solution)/shard_map/ppermute | solution.py:19
  7.5 23.3 %collective-permute-start.1 = (bf16[192,128]{1,0:T(8,128)(2,1)S(1)}, bf16[192,128]{1,0:T(8,128)(2,1)S(1)}, u32[]{:S(2)}, u32[]{:S(2)}) collective-permute-start(bf16[192,128]{1,0:T(8,128)(2,1)S(1)} %get-tuple-element.292), channel_id=1, source_target_pairs={{2,0},{3,1},{4,2},{5,3},{6,4},{7,5},{8,6},{9,7},{10,8},{11,9},{12,... | collective-permute-start | bytes 147464 | tf_op jit(solution)/shard_map/ppermute | solution.py:19
  8.1 22.7 %collective-permute-start.2 = (bf16[192,128]{1,0:T(8,128)(2,1)S(1)}, bf16[192,128]{1,0:T(8,128)(2,1)S(1)}, u32[]{:S(2)}, u32[]{:S(2)}) collective-permute-start(bf16[192,128]{1,0:T(8,128)(2,1)S(1)} %get-tuple-element.291), channel_id=1, source_target_pairs={{3,0},{4,1},{5,2},{6,3},{7,4},{8,5},{9,6},{10,7},{11,8},{12,9},{13... | collective-permute-start | bytes 147464 | tf_op jit(solution)/shard_map/ppermute | solution.py:19
  8.4 25.0 %collective-permute-start.3 = (bf16[192,128]{1,0:T(8,128)(2,1)S(1)}, bf16[192,128]{1,0:T(8,128)(2,1)S(1)}, u32[]{:S(2)}, u32[]{:S(2)}) collective-permute-start(bf16[192,128]{1,0:T(8,128)(2,1)S(1)} %get-tuple-element.290), channel_id=1, source_target_pairs={{4,0},{5,1},{6,2},{7,3},{8,4},{9,5},{10,6},{11,7},{12,8},{13,9},{1... | collective-permute-start | bytes 147464 | tf_op jit(solution)/shard_map/ppermute | solution.py:19
  8.8 25.1 %collective-permute-start.4 = (bf16[192,128]{1,0:T(8,128)(2,1)S(1)}, bf16[192,128]{1,0:T(8,128)(2,1)S(1)}, u32[]{:S(2)}, u32[]{:S(2)}) collective-permute-start(bf16[192,128]{1,0:T(8,128)(2,1)S(1)} %get-tuple-element.289), channel_id=1, source_target_pairs={{5,0},{6,1},{7,2},{8,3},{9,4},{10,5},{11,6},{12,7},{13,8},{14,9},{... | collective-permute-start | bytes 147464 | tf_op jit(solution)/shard_map/ppermute | solution.py:19
  10.5 13.1 %all-to-all-start = ((f32[16,1,2]{2,1,0:T(1,128)}), f32[16,1,2]{2,1,0:T(1,128)S(1)}, u32[]{:S(2)}, u32[]{:S(2)}) async-start(f32[16,1,2]{2,1,0:T(1,128)} %bitcast.45), calls=%async_computation | async-start | bytes 16384 | tf_op jit(solution)/shard_map/all_to_all | solution.py:132
  23.5 197.2 %all-to-all-start.2 = ((f32[16,2,8]{2,1,0:T(2,128)}), f32[16,2,8]{2,1,0:T(2,128)S(1)}, u32[]{:S(2)}, u32[]{:S(2)}) async-start(f32[16,2,8]{2,1,0:T(2,128)} %bitcast.51), calls=%async_computation.2 | async-start | bytes 32768 | tf_op jit(solution)/shard_map/all_to_all | solution.py:131
  27.1 9.3 %collective-permute-start.5 = (bf16[192,128]{1,0:T(8,128)(2,1)S(1)}, bf16[192,128]{1,0:T(8,128)(2,1)S(1)}, u32[]{:S(2)}, u32[]{:S(2)}) collective-permute-start(bf16[192,128]{1,0:T(8,128)(2,1)S(1)} %get-tuple-element.288), channel_id=1, source_target_pairs={{6,0},{7,1},{8,2},{9,3},{10,4},{11,5},{12,6},{13,7},{14,8},{15,9},... | collective-permute-start | bytes 147464 | tf_op jit(solution)/shard_map/ppermute | solution.py:19
  30.8 6.6 %collective-permute-start.6 = (bf16[192,128]{1,0:T(8,128)(2,1)S(1)}, bf16[192,128]{1,0:T(8,128)(2,1)S(1)}, u32[]{:S(2)}, u32[]{:S(2)}) collective-permute-start(bf16[192,128]{1,0:T(8,128)(2,1)S(1)} %get-tuple-element.287), channel_id=1, source_target_pairs={{7,0},{8,1},{9,2},{10,3},{11,4},{12,5},{13,6},{14,7},{15,8},{0,9},... | collective-permute-start | bytes 147464 | tf_op jit(solution)/shard_map/ppermute | solution.py:19
  30.9 8.5 %collective-permute-start.7 = (bf16[192,128]{1,0:T(8,128)(2,1)S(1)}, bf16[192,128]{1,0:T(8,128)(2,1)S(1)}, u32[]{:S(2)}, u32[]{:S(2)}) collective-permute-start(bf16[192,128]{1,0:T(8,128)(2,1)S(1)} %get-tuple-element.286), channel_id=1, source_target_pairs={{8,0},{9,1},{10,2},{11,3},{12,4},{13,5},{14,6},{15,7},{0,8},{1,9},... | collective-permute-start | bytes 147464 | tf_op jit(solution)/shard_map/ppermute | solution.py:19
  33.4 7.7 %collective-permute-start.8 = (bf16[192,128]{1,0:T(8,128)(2,1)S(1)}, bf16[192,128]{1,0:T(8,128)(2,1)S(1)}, u32[]{:S(2)}, u32[]{:S(2)}) collective-permute-start(bf16[192,128]{1,0:T(8,128)(2,1)S(1)} %get-tuple-element.285), channel_id=1, source_target_pairs={{9,0},{10,1},{11,2},{12,3},{13,4},{14,5},{15,6},{0,7},{1,8},{2,9},... | collective-permute-start | bytes 147464 | tf_op jit(solution)/shard_map/ppermute | solution.py:19
  33.9 11.3 %collective-permute-start.9 = (bf16[192,128]{1,0:T(8,128)(2,1)S(1)}, bf16[192,128]{1,0:T(8,128)(2,1)S(1)}, u32[]{:S(2)}, u32[]{:S(2)}) collective-permute-start(bf16[192,128]{1,0:T(8,128)(2,1)S(1)} %get-tuple-element.284), channel_id=1, source_target_pairs={{10,0},{11,1},{12,2},{13,3},{14,4},{15,5},{0,6},{1,7},{2,8},{3,9},... | collective-permute-start | bytes 147464 | tf_op jit(solution)/shard_map/ppermute | solution.py:19
  36.4 10.3 %collective-permute-start.10 = (bf16[192,128]{1,0:T(8,128)(2,1)S(1)}, bf16[192,128]{1,0:T(8,128)(2,1)S(1)}, u32[]{:S(2)}, u32[]{:S(2)}) collective-permute-start(bf16[192,128]{1,0:T(8,128)(2,1)S(1)} %get-tuple-element.283), channel_id=1, source_target_pairs={{11,0},{12,1},{13,2},{14,3},{15,4},{0,5},{1,6},{2,7},{3,8},{4,9},{... | collective-permute-start | bytes 147464 | tf_op jit(solution)/shard_map/ppermute | solution.py:19
  37.4 9.3 %collective-permute-start.11 = (bf16[192,128]{1,0:T(8,128)(2,1)S(1)}, bf16[192,128]{1,0:T(8,128)(2,1)S(1)}, u32[]{:S(2)}, u32[]{:S(2)}) collective-permute-start(bf16[192,128]{1,0:T(8,128)(2,1)S(1)} %get-tuple-element.282), channel_id=1, source_target_pairs={{12,0},{13,1},{14,2},{15,3},{0,4},{1,5},{2,6},{3,7},{4,8},{5,9},{6... | collective-permute-start | bytes 147464 | tf_op jit(solution)/shard_map/ppermute | solution.py:19
  39.4 7.4 %collective-permute-start.12 = (bf16[192,128]{1,0:T(8,128)(2,1)S(1)}, bf16[192,128]{1,0:T(8,128)(2,1)S(1)}, u32[]{:S(2)}, u32[]{:S(2)}) collective-permute-start(bf16[192,128]{1,0:T(8,128)(2,1)S(1)} %get-tuple-element.281), channel_id=1, source_target_pairs={{13,0},{14,1},{15,2},{0,3},{1,4},{2,5},{3,6},{4,7},{5,8},{6,9},{7,... | collective-permute-start | bytes 147464 | tf_op jit(solution)/shard_map/ppermute | solution.py:19
  41.1 7.1 %collective-permute-start.13 = (bf16[192,128]{1,0:T(8,128)(2,1)S(1)}, bf16[192,128]{1,0:T(8,128)(2,1)S(1)}, u32[]{:S(2)}, u32[]{:S(2)}) collective-permute-start(bf16[192,128]{1,0:T(8,128)(2,1)S(1)} %get-tuple-element.295), channel_id=1, source_target_pairs={{14,0},{15,1},{0,2},{1,3},{2,4},{3,5},{4,6},{5,7},{6,8},{7,9},{8,1... | collective-permute-start | bytes 147464 | tf_op jit(solution)/shard_map/ppermute | solution.py:19
  45.2 6.2 %collective-permute-start.14 = (bf16[192,128]{1,0:T(8,128)(2,1)S(1)}, bf16[192,128]{1,0:T(8,128)(2,1)S(1)}, u32[]{:S(2)}, u32[]{:S(2)}) collective-permute-start(bf16[192,128]{1,0:T(8,128)(2,1)S(1)} %get-tuple-element.280), channel_id=1, source_target_pairs={{15,0},{0,1},{1,2},{2,3},{3,4},{4,5},{5,6},{6,7},{7,8},{8,9},{9,10... | collective-permute-start | bytes 147464 | tf_op jit(solution)/shard_map/ppermute | solution.py:19
  65.7 6.5 %copy-start.5 = (bf16[16,192,128]{2,1,0:T(8,128)(2,1)S(1)}, bf16[16,192,128]{2,1,0:T(8,128)(2,1)}, u32[]{:S(2)}) copy-start(bf16[16,192,128]{2,1,0:T(8,128)(2,1)} %copy-done.4) | copy-start | bytes 2359300 | tf_op jit(solution)/shard_map/while
  76.1 6.5 %copy-start.5 = (bf16[16,192,128]{2,1,0:T(8,128)(2,1)S(1)}, bf16[16,192,128]{2,1,0:T(8,128)(2,1)}, u32[]{:S(2)}) copy-start(bf16[16,192,128]{2,1,0:T(8,128)(2,1)} %copy-done.4) | copy-start | bytes 2359300 | tf_op jit(solution)/shard_map/while
  128.3 6.5 %copy-start.5 = (bf16[16,192,128]{2,1,0:T(8,128)(2,1)S(1)}, bf16[16,192,128]{2,1,0:T(8,128)(2,1)}, u32[]{:S(2)}) copy-start(bf16[16,192,128]{2,1,0:T(8,128)(2,1)} %copy-done.4) | copy-start | bytes 2359300 | tf_op jit(solution)/shard_map/while
  218.2 20.2 %copy-start = (f32[192,128]{1,0:T(8,128)}, f32[192,128]{1,0:T(8,128)S(1)}, u32[]{:S(2)}) copy-start(f32[192,128]{1,0:T(8,128)S(1)} %get-tuple-element.221) | copy-start | bytes 294916
  220.7 11.4 %all-to-all-start.1 = ((f32[16,2,8,128]{3,1,2,0:T(2,128)}), f32[16,2,8,128]{3,1,2,0:T(2,128)S(1)}, u32[]{:S(2)}, u32[]{:S(2)}) async-start(f32[16,2,8,128]{3,1,2,0:T(2,128)} %copy.36), calls=%async_computation.1 | async-start | bytes 262144 | tf_op jit(solution)/shard_map/all_to_all | solution.py:130
  232.4 4.3 %collective-permute-start.15 = (f32[1,128]{1,0:T(1,128)S(1)}, f32[1,128]{1,0:T(1,128)S(1)}, u32[]{:S(2)}, u32[]{:S(2)}) collective-permute-start(f32[1,128]{1,0:T(1,128)S(1)} %get-tuple-element.297), channel_id=1, source_target_pairs={{1,0},{2,1},{3,2},{4,3},{5,4},{6,5},{7,6},{8,7},{9,8},{10,9},{11,1... | collective-permute-start | bytes 1544 | tf_op jit(solution)/shard_map/ppermute | solution.py:30
  233.7 3.8 %collective-permute-start.16 = (f32[1,128]{1,0:T(1,128)S(1)}, f32[1,128]{1,0:T(1,128)S(1)}, u32[]{:S(2)}, u32[]{:S(2)}) collective-permute-start(f32[1,128]{1,0:T(1,128)S(1)} %get-tuple-element.296), channel_id=1, source_target_pairs={{0,1},{1,2},{2,3},{3,4},{4,5},{5,6},{6,7},{7,8},{8,9},{9,10},{10,1... | collective-permute-start | bytes 1544 | tf_op jit(solution)/shard_map/ppermute | solution.py:27
  (29 other events, 98.9 us)
where the time goes:
time: 242 us; the launch traced here: 238 us
  matrix products  69.3 us (29%)
  local copies, waits for them, and re-layouts  58.2 us (24%)
  other arithmetic  46.3 us (19%)
  starting transfers between devices  40.2 us (17%)
  waiting for transfers between devices  21.8 us (9%)
    dot_general x16, matrix products, visit_view(): jnp.einsum('rij,rjk->ik', kernel_xy, along_z, preferred_element_type=jnp....  31.5 us
    convert_element_type x16, local copies, waits for them, and re-layouts, kron_rows(): outer.reshape(outer.shape[:-4] + (rows_xy, rows_xy)).astype(jnp.bfloat16)  29.4 us
    ppermute x15, starting transfers between devices, from_behind(): return lax.ppermute(block, axis, route)  22.2 us
    dot_general x16, matrix products, visit_view(): jnp.einsum('rji,rjz->iz', kernel_xy, back_z, preferred_element_type=jnp.f...  20.8 us
    reduce_sum x16, other arithmetic, visit_view(): column_xy = jnp.sum(kernel_xy.astype(jnp.float32), axis=1)  18.3 us
    dot_general x16, matrix products, visit_view(): jnp.einsum('ri,rz->iz', column_xy, column_z, precision=lax.Precision.HIGH...  16.4 us
    reduce_sum x16, other arithmetic, visit_view(): column_z = jnp.sum(kernel_z.astype(jnp.float32), axis=1)  14.8 us
    convert_element_type x16, other arithmetic, kron_rows(): kernel_y.astype(jnp.float32)[..., None, :, None, :]  11.9 us
  transfers between devices with their start and end apart: 20, of which 7 were waited for; matrix products, arithmetic and copies ran while one was open for 71% of the time, Pallas kernels for 0%

commit v1 on v0

v1 whole, which is shorter than its diff:
```python
import functools

import jax
import jax.numpy as jnp
from jax import lax
from jax.experimental import pallas as pl
from jax.experimental.pallas import tpu as pltpu
from jax.sharding import PartitionSpec as P

SROWS = 8
TROWS = 64
CAP = 2
EDGE = CAP * SROWS
META = EDGE + 2
SLOT = 24
OFFSETS = CAP * SROWS
EDGE_WEIGHTS = OFFSETS + CAP

smooth_rate = 0.24
edge_scale = 1.0

f32 = jnp.float32
bf16 = jnp.bfloat16
VMEM = pl.BlockSpec(memory_space=pltpu.VMEM)
SMEM = pl.BlockSpec(memory_space=pltpu.SMEM)
ANY = pl.BlockSpec(memory_space=pl.ANY)


def dot(a, b):
    return jnp.dot(a, b, preferred_element_type=f32)


def by_target_kernel(place_ref, source_ref, target_ref, sems):
    count = target_ref.shape[0]
    copies = []
    for target in range(count):
        stop_id = lax.rem(place_ref[0] + count - target, count)
        copies.append(
            pltpu.make_async_copy(source_ref.at[stop_id], target_ref.at[target], sems.at[target])
        )
    for copy in copies:
        copy.start()
    for copy in copies:
        copy.wait()


def by_target(measured, place):
    return pl.pallas_call(
        by_target_kernel,
        out_shape=jax.ShapeDtypeStruct(measured.shape, measured.dtype),
        in_specs=[SMEM, ANY],
        out_specs=ANY,
        scratch_shapes=[pltpu.SemaphoreType.DMA((measured.shape[0],))],
    )(place, measured)


def prepare_kernel(
    x_ref, y_ref, back_x_ref, back_y_ref, spread_x_ref, spread_y_ref, z_ref, front_ref, back_ref, log_ref
):
    rank = z_ref.shape[1]
    for wide_x, wide_y, target_ref in (
        (x_ref, y_ref, front_ref),
        (back_x_ref, back_y_ref, back_ref),
    ):
        lines_x = dot(wide_x[0], spread_x_ref[...])
        lines_y = dot(wide_y[0], spread_y_ref[...])
        extent_y = lines_y.shape[0]
        for x in range(lines_x.shape[0]):
            target_ref[0, x * extent_y : (x + 1) * extent_y, :] = (
                lines_x[x : x + 1, :] * lines_y
            ).astype(bf16)
    lines = back_ref.shape[1]
    depth = z_ref.shape[3]
    ones = jnp.ones((lines, depth), bf16)
    total = jnp.zeros((lines, depth), f32)
    for r in range(rank):
        column_xy = dot(back_ref[0, :, r * lines : (r + 1) * lines], ones)
        column_z = jnp.sum(z_ref[0, r].astype(f32), axis=0, keepdims=True)
        total = total + column_xy * column_z
    log_ref[0] = jnp.log(total)


def prepare(kernel_x, kernel_y, kernel_z):
    views, rank, extent_x, _ = kernel_x.shape
    extent_y = kernel_y.shape[2]
    depth = kernel_z.shape[3]
    lines = extent_x * extent_y
    wide = rank * lines
    column = jnp.arange(wide, dtype=jnp.int32)
    part, inner = column // lines, column % lines
    rows_x = jnp.arange(rank * extent_x, dtype=jnp.int32)[:, None]
    rows_y = jnp.arange(rank * extent_y, dtype=jnp.int32)[:, None]
    spread_x = (rows_x == part * extent_x + inner // extent_y).astype(bf16)
    spread_y = (rows_y == part * extent_y + inner % extent_y).astype(bf16)
    front_x = kernel_x.transpose(0, 2, 1, 3).reshape(views, extent_x, rank * extent_x)
    front_y = kernel_y.transpose(0, 2, 1, 3).reshape(views, extent_y, rank * extent_y)
    back_x = kernel_x.transpose(0, 3, 1, 2).reshape(views, extent_x, rank * extent_x)
    back_y = kernel_y.transpose(0, 3, 1, 2).reshape(views, extent_y, rank * extent_y)

    def of_view(shape):
        return pl.BlockSpec((1,) + shape, lambda v: (v,) + (0,) * len(shape))

    def whole(array):
        return pl.BlockSpec(array.shape, lambda v: (0,) * array.ndim)

    return pl.pallas_call(
        prepare_kernel,
        grid=(views,),
        out_shape=(
            jax.ShapeDtypeStruct((views, lines, wide), bf16),
            jax.ShapeDtypeStruct((views, lines, wide), bf16),
            jax.ShapeDtypeStruct((views, lines, depth), f32),
        ),
        in_specs=[
            of_view(front_x.shape[1:]),
            of_view(front_y.shape[1:]),
            of_view(back_x.shape[1:]),
            of_view(back_y.shape[1:]),
            whole(spread_x),
            whole(spread_y),
            of_view(kernel_z.shape[1:]),
        ],
        out_specs=(of_view((lines, wide)), of_view((lines, wide)), of_view((lines, depth))),
        cost_estimate=pl.CostEstimate(
            flops=views * 8 * lines * wide, bytes_accessed=views * 8 * lines * wide, transcendentals=0
        ),
    )(front_x, front_y, back_x, back_y, spread_x, spread_y, kernel_z)


def stops_kernel(
    view_ref,
    record_ref,
    background_ref,
    relax_ref,
    slot_ref,
    owner_ref,
    source_ref,
    tile_ref,
    estimate_ref,
    weight_ref,
    meta_ref,
    front_hbm,
    back_hbm,
    toward_hbm,
    z_hbm,
    log_hbm,
    records_hbm,
    refined_ref,
    send_ref,
    front_ref,
    back_ref,
    toward_ref,
    z_ref,
    log_ref,
    records_ref,
    sems,
):
    stops = records_ref.shape[0]
    targets = send_ref.shape[0]
    rank = z_ref.shape[1] // z_ref.shape[2]
    depth = z_ref.shape[2]

    def copies(stop_id):
        view_id = view_ref[stop_id]
        pairs = (
            (toward_hbm.at[view_id], toward_ref),
            (front_hbm.at[view_id], front_ref),
            (records_hbm.at[record_ref[stop_id]], records_ref),
            (z_hbm.at[view_id], z_ref),
            (back_hbm.at[view_id], back_ref),
            (log_hbm.at[view_id], log_ref),
        )
        return [
            pltpu.make_async_copy(source, target.at[stop_id], sems.at[k, stop_id])
            for k, (source, target) in enumerate(pairs)
        ]

    ahead = min(2, stops)
    for stop_id in range(ahead):
        for copy in copies(stop_id):
            copy.start()

    def parts(factors, lines):
        return jnp.concatenate(
            [dot(lines, factors[r * depth : (r + 1) * depth]).astype(bf16) for r in range(rank)],
            axis=0,
        )

    def advance(stop_id, block):
        @pl.when(stop_id + ahead < stops)
        def _():
            for copy in copies(stop_id + ahead):
                copy.start()

        for copy in copies(stop_id):
            copy.wait()
        view_id = view_ref[stop_id]
        along_z = parts(toward_ref[stop_id], block.astype(bf16))
        forward = dot(front_ref[stop_id], along_z)
        ratio = (records_ref[stop_id].astype(f32) / (forward + background_ref[view_id])).astype(bf16)
        back_z = parts(z_ref[stop_id], ratio)
        adjoint = dot(back_ref[stop_id], back_z)
        return block * jnp.exp(relax_ref[view_id] * (jnp.log(adjoint) - log_ref[stop_id]))

    refined_ref[...] = lax.fori_loop(0, stops, advance, estimate_ref[...])

    send_ref[:, :EDGE, :] = jnp.zeros((targets, EDGE, depth), f32)
    send_ref[:, EDGE:, :] = meta_ref[...]

    def place(entry, carried):
        owner, tile = owner_ref[entry], tile_ref[entry]
        slot = slot_ref[entry]
        piece = refined_ref[pl.ds(source_ref[entry], SROWS), :] * weight_ref[entry]
        row = pl.multiple_of(lax.rem(slot, CAP) * SROWS, SROWS)
        send_ref[owner, pl.ds(row, SROWS), :] = piece

        @pl.when((tile == TROWS - SROWS) & (owner + 1 < targets))
        def _():
            send_ref[owner + 1, EDGE : EDGE + 1, :] += piece[SROWS - 1 :]

        @pl.when((tile == 0) & (owner > 0))
        def _():
            send_ref[owner - 1, EDGE + 1 : EDGE + 2, :] += piece[:1]

        return carried

    lax.fori_loop(0, source_ref.shape[0], place, 0)


def run_stops(scalars, estimate, weights, meta, front, back, toward, kernel_z, logs, records):
    lines, depth = estimate.shape
    stops = records.shape[0]
    targets = meta.shape[0]
    staged = (front, back, toward, kernel_z, logs, records)
    return pl.pallas_call(
        stops_kernel,
        out_shape=(
            jax.ShapeDtypeStruct((lines, depth), f32),
            jax.ShapeDtypeStruct((targets, SLOT, depth), f32),
        ),
        in_specs=[SMEM] * len(scalars) + [VMEM] * 3 + [ANY] * len(staged),
        out_specs=(VMEM, VMEM),
        scratch_shapes=[pltpu.VMEM((stops,) + a.shape[1:], a.dtype) for a in staged]
        + [pltpu.SemaphoreType.DMA((len(staged), stops))],
        compiler_params=pltpu.CompilerParams(vmem_limit_bytes=32 << 20),
    )(*scalars, estimate, weights, meta, *staged)


def blend_kernel(place_ref, data_ref, smoothed_ref):
    count, _, depth = data_ref.shape
    place = place_ref[0]
    slots = count * EDGE
    meta = data_ref[:, META, :]
    key = lax.broadcasted_iota(jnp.int32, (depth, slots), 0)
    column = lax.broadcasted_iota(jnp.int32, (depth, slots), 1) % EDGE
    spread_weight = (key == column).astype(bf16)
    spread_offset = (key == OFFSETS + column // SROWS).astype(bf16)
    own = lax.broadcasted_iota(jnp.int32, (count, slots), 0) == (
        lax.broadcasted_iota(jnp.int32, (count, slots), 1) // EDGE
    )
    coded = meta.astype(bf16)
    weight = jnp.sum(jnp.where(own, dot(coded, spread_weight), 0.0), axis=0, keepdims=True)
    offset = jnp.sum(jnp.where(own, dot(coded, spread_offset), 0.0), axis=0, keepdims=True)
    line = offset.astype(jnp.int32) + lax.broadcasted_iota(jnp.int32, (1, slots), 1) % SROWS
    placed = (line == lax.broadcasted_iota(jnp.int32, (TROWS, slots), 0)).astype(f32)
    data = data_ref[:, :EDGE, :].reshape(slots, depth)
    numerator = 1.0 + jnp.dot(
        placed, data, preferred_element_type=f32, precision=lax.Precision.HIGHEST
    )
    denominator = 1.0 + jnp.sum(placed * weight, axis=1, keepdims=True)
    joined = numerator / denominator

    def edge(which, inside):
        top = 1.0 + jnp.sum(data_ref[:, EDGE + which, :], axis=0, keepdims=True)
        lane = EDGE_WEIGHTS + which
        below = 1.0 + jnp.sum(meta[:, lane : lane + 1], axis=0, keepdims=True)
        return jnp.where(inside, top / below, 0.0)

    behind = edge(0, place > 0)
    beyond = edge(1, place < count - 1)
    side = jnp.zeros((TROWS, 1), f32)
    flux = jnp.zeros_like(joined)
    for neighbor in (
        jnp.concatenate([joined[1:], beyond], axis=0),
        jnp.concatenate([behind, joined[:-1]], axis=0),
        jnp.concatenate([joined[:, 1:], side], axis=1),
        jnp.concatenate([side, joined[:, :-1]], axis=1),
    ):
        change = neighbor - joined
        flux = flux + change / (1.0 + change / edge_scale * (change / edge_scale))
    smoothed_ref[...] = joined + smooth_rate * flux


def blend(place, data):
    return pl.pallas_call(
        blend_kernel,
        out_shape=jax.ShapeDtypeStruct((TROWS, data.shape[2]), f32),
        in_specs=[SMEM, VMEM],
        out_specs=VMEM,
        compiler_params=pltpu.CompilerParams(vmem_limit_bytes=32 << 20),
    )(place, data)


def listing(owner, tile_offset, feather, targets):
    listed = owner.shape[0]
    entry_ids = jnp.arange(listed, dtype=jnp.int32)
    earlier = (owner[:, None] == owner[None, :]) & (entry_ids[None, :] < entry_ids[:, None])
    slot_ids = owner * CAP + jnp.sum(earlier.astype(jnp.int32), axis=1)
    weights = feather.astype(f32)
    slots = jnp.arange(targets * CAP, dtype=jnp.int32)[:, None]
    taken = (slots == slot_ids[None, :]).astype(f32)
    slot_weights = jnp.sum(taken[:, :, None] * weights[None], axis=1).reshape(targets, CAP * SROWS)
    slot_offsets = jnp.sum(taken * tile_offset.astype(f32)[None], axis=1).reshape(targets, CAP)
    tiles = jnp.arange(targets, dtype=jnp.int32)[:, None]
    last = (owner[None] + 1 == tiles) & (tile_offset[None] == TROWS - SROWS)
    first = (owner[None] - 1 == tiles) & (tile_offset[None] == 0)
    edge_weights = [
        jnp.sum(jnp.where(reached, weights[None, :, q], 0.0), axis=1, keepdims=True)
        for reached, q in ((last, SROWS - 1), (first, 0))
    ]
    row = jnp.concatenate([slot_weights, slot_offsets] + edge_weights, axis=1)
    return slot_ids, weights, row


def on_device(
    estimate,
    measured,
    kernel_z,
    kernel_x,
    kernel_y,
    background,
    relax,
    owner,
    source_offset,
    tile_offset,
    feather,
):
    count = lax.axis_size("view")
    position = lax.axis_index("view").astype(jnp.int32)
    place = position.reshape(1)
    stops = measured.shape[0]
    views, rank, depth, _ = kernel_z.shape
    stop_ids = jnp.arange(stops, dtype=jnp.int32)
    hosts = (position + stop_ids) % count
    view_ids = hosts % views
    if stops == count:
        records = lax.all_to_all(
            by_target(measured, place), "view", split_axis=0, concat_axis=0, tiled=True
        )
        record_ids = hosts
    else:
        arrived = [measured[0]]
        for stop_id in range(1, stops):
            route = [((i + stop_id) % count, i) for i in range(count)]
            arrived.append(lax.ppermute(measured[stop_id], "view", route))
        records = jnp.stack(arrived, axis=0)
        record_ids = stop_ids

    front, back, logs = prepare(kernel_x, kernel_y, kernel_z)
    toward = kernel_z.swapaxes(2, 3).reshape(views, rank * depth, depth)
    owner = owner[:, 0]
    slot_ids, weights, row = listing(owner, tile_offset, feather, count)
    meta = jnp.zeros((count, SLOT - EDGE, depth), f32).at[:, META - EDGE, : row.shape[1]].set(row)
    weights = jnp.broadcast_to(weights[:, :, None], weights.shape + (depth,))
    scalars = (
        view_ids,
        record_ids,
        background.astype(f32),
        relax.astype(f32),
        slot_ids,
        owner,
        source_offset,
        tile_offset,
    )
    refined, outgoing = run_stops(
        scalars,
        estimate,
        weights,
        meta,
        front,
        back,
        toward,
        kernel_z.reshape(views, rank * depth, depth),
        logs,
        records,
    )
    incoming = lax.all_to_all(outgoing, "view", split_axis=0, concat_axis=0, tiled=True)
    return refined, blend(place, incoming)


def solution(mesh):
    lined = P(("groups", "view"))
    return jax.shard_map(
        on_device,
        mesh=mesh,
        in_specs=(
            P(("groups", "view"), None),
            P(("groups", "view"), None, None),
            P(),
            P(),
            P(),
            P(),
            P(),
            P(("groups", "view"), None),
            lined,
            lined,
            P(("groups", "view"), None),
        ),
        out_specs=(P(("groups", "view"), None), P(("groups", "view"), None)),
        check_vma=False,
    )
```

time: 242 us -> 107 us (0.44); the launches traced: 238 us -> 106 us
  Pallas kernels: 0 us -> 70.2 us
  matrix products: 69.3 us -> 0 us
  local copies, waits for them, and re-layouts: 58.2 us -> 10.6 us
  other arithmetic: 46.3 us -> 1.96 us
  starting transfers between devices: 40.2 us -> 7.57 us
  waiting for transfers between devices: 21.8 us -> 0.01 us
  blocking collectives: 0 us -> 14.8 us
    pallas_call x0 -> x4, Pallas kernels: none -> 70.2 us  [the longest x1 31.1 us: run_stops(): pl.pallas_call(stops_kernel, out_shape=(jax.ShapeDtypeStruct((lines, dept...]
    dot_general x50 -> x0, matrix products: 69.3 us -> none  [the longest x16 31.5 us: visit_view(): jnp.einsum('rij,rjk->ik', kernel_xy, along_z, preferred_element_type=jnp....]
    reduce_sum x33 -> x4, other arithmetic: 33.3 us -> 0.47 us  [the longest x1 0.18 us: listing(): slot_ids = owner * CAP + jnp.sum(earlier.astype(jnp.int32), axis=1)]
    convert_element_type x17 -> x1, local copies, waits for them, and re-layouts: 29.5 us -> 0.07 us  [listing(): weights = feather.astype(f32)]
    ppermute x17 -> x0, starting transfers between devices: 26.5 us -> none  [the longest x15 22.2 us: from_behind(): return lax.ppermute(block, axis, route)]
    dynamic_slice x32 -> x0, local copies, waits for them, and re-layouts: 18.8 us -> none  [the longest x16 9.42 us: advance(): back_values[view_id]]
    all_to_all x0 -> x1, blocking collectives: none -> 14.8 us  [on_device(): lax.all_to_all(outgoing, 'view', split_axis=0, concat_axis=0, tiled=True)]
    all_to_all x3 -> x1, waiting for transfers between devices: 12.2 us -> 0.01 us  [on_device(): lax.all_to_all(by_target(measured, place), 'view', split_axis=0, concat_a...]
  transfers between devices with their start and end apart: 20 -> 1, of which waited for: 7 -> 0; matrix products, arithmetic and copies ran while one was open for 71% -> 6% of each run, Pallas kernels for 0% -> 12%
where the time goes in v1:
time: 107 us; the launch traced here: 106 us
  Pallas kernels  70.2 us (66%)
  blocking collectives  14.8 us (14%)
  local copies, waits for them, and re-layouts  10.6 us (10%)
  starting transfers between devices  7.57 us (7%)
  other arithmetic  1.96 us (2%)
    pallas_call x1, Pallas kernels, run_stops(): pl.pallas_call(stops_kernel, out_shape=(jax.ShapeDtypeStruct((lines, dept...  31.1 us
    pallas_call x1, Pallas kernels, by_target(): pl.pallas_call(by_target_kernel, out_shape=jax.ShapeDtypeStruct(measured....  25.1 us
    all_to_all x1, blocking collectives, on_device(): lax.all_to_all(outgoing, 'view', split_axis=0, concat_axis=0, tiled=True)  14.8 us
    pallas_call x1, Pallas kernels, prepare(): pl.pallas_call(prepare_kernel, grid=(views,), out_shape=(jax.ShapeDtypeSt...  12.9 us
    all_to_all x1, starting transfers between devices, on_device(): lax.all_to_all(by_target(measured, place), 'view', split_axis=0, concat_a...  7.57 us
    unnamed x28, local copies, waits for them, and re-layouts  5.69 us
  transfers between devices with their start and end apart: 1, of which 0 were waited for; matrix products, arithmetic and copies ran while one was open for 6% of the time, Pallas kernels for 12%

profile of v1, /device:TPU:0, one launch (start us, length us, event | category | flops | bytes accessed | tf_op | source)
XLA Modules:
  0.0 105.9 jit_solution(13445318465469136469)
XLA Ops:
  0.7 25.1 %shard_map.123 = bf16[16,192,128]{2,1,0:T(8,128)(2,1)} custom-call(s32[1]{0:T(128)} %bitcast.15.place_ref, bf16[16,192,128]{2,1,0:T(8,128)(2,1)} %source_ref.2), custom_call_target="tpu_custom_call" | custom-call | tf_op jit(solution)/shard_map/pallas_call | solution.py:48
  25.8 7.6 %all-to-all-start = ((bf16[16,192,128]{2,1,0:T(8,128)(2,1)}), bf16[16,192,128]{2,1,0:T(8,128)(2,1)}, u32[]{:S(2)}, u32[]{:S(2)}) async-start(bf16[16,192,128]{2,1,0:T(8,128)(2,1)} %shard_map.123), calls=%async_computation | async-start | bytes 1572864 | tf_op jit(solution)/shard_map/all_to_all | solution.py:347
  33.4 0.2 convert_reduce_fusion
  33.6 0.1 copy.33
  33.7 0.1 select_reduce_fusion
  33.8 0.1 copy.36
  33.9 0.1 copy.37
  34.0 0.1 fusion.6
  34.0 0.1 multiply_reduce_fusion
  34.1 0.1 copy.35
  34.2 0.1 reshape.172
  34.3 0.1 select_reduce_fusion.2
  34.4 0.1 reshape.173
  34.5 0.0 copy-done.9
  34.5 0.1 copy.39
  34.6 0.8 reshape.176.y_ref
  35.4 0.1 copy.45
  35.5 0.8 reshape.182.x_ref
  36.3 0.9 copy.43.back_x_ref
  37.2 0.7 copy.48.back_y_ref
  37.9 0.9 copy.44
  38.9 0.1 pad_maximum_fusion
  39.0 0.6 fusion.1.spread_x_ref
  39.7 0.6 fusion.spread_y_ref
  40.3 12.9 %shard_map.122 = (bf16[16,192,576]{2,1,0:T(8,128)(2,1)}, bf16[16,192,576]{2,1,0:T(8,128)(2,1)}, f32[16,192,128]{2,1,0:T(8,128)}) custom-call(bf16[16,12,36]{2,1,0:T(8,128)(2,1)} %reshape.182.x_ref, bf16[16,16,48]{2,1,0:T(8,128)(2,1)} %reshape.176.y_ref, bf16[16,12,36]{2,1,0:T(8,128)(2,1)} %copy.43.back_x_ref, bf16[16,16,48]{2,1,0:T(8,128)(2,1)} %copy.48.back_y_ref, ...), custom_call_target="tpu_custom_call" | custom-call | flops 14155776 | bytes 14155776 | tf_op jit(solution)/shard_map/pallas_call | solution.py:106
  53.2 0.1 broadcast_in_dim.28.weight_ref
  53.3 2.1 %copy-done.2 = bf16[16,192,576]{2,1,0:T(8,128)(2,1)S(1)} copy-done((bf16[16,192,576]{2,1,0:T(8,128)(2,1)S(1)}, bf16[16,192,576]{2,1,0:T(8,128)(2,1)}, u32[]{:S(2)}) %copy-start.2) | copy-done | bytes 3538968
  55.5 2.1 %copy-done.3 = bf16[16,192,576]{2,1,0:T(8,128)(2,1)S(1)} copy-done((bf16[16,192,576]{2,1,0:T(8,128)(2,1)S(1)}, bf16[16,192,576]{2,1,0:T(8,128)(2,1)}, u32[]{:S(2)}) %copy-start.3) | copy-done | bytes 3538968
  57.6 1.4 %copy-done.4 = f32[16,192,128]{2,1,0:T(8,128)S(1)} copy-done((f32[16,192,128]{2,1,0:T(8,128)S(1)}, f32[16,192,128]{2,1,0:T(8,128)}, u32[]{:S(2)}) %copy-start.4) | copy-done | bytes 1572888
  59.0 31.1 %shard_map.124 = (f32[192,128]{1,0:T(8,128)}, f32[16,24,128]{2,1,0:T(8,128)S(1)}) custom-call(s32[16]{0:T(128)S(1)} %get-tuple-element.31.view_ref, s32[16]{0:T(128)S(1)} %get-tuple-element.32.record_ref, f32[16]{0:T(128)S(1)} %convert_element_type.28.background_ref, f32[16]{0:T(128)S(1)} %convert_element_type.29.relax_ref, ...), custom_call_target="tpu_custom_call" | custom-call | tf_op jit(solution)/shard_map/pallas_call | solution.py:235
  90.1 14.8 %all_to_all.10.data_ref = f32[16,24,128]{2,1,0:T(8,128)S(1)} all-to-all(f32[16,24,128]{2,1,0:T(8,128)S(1)} %get-tuple-element.23), channel_id=1, replica_groups=mesh['groups'=2,'view'=16] {'view'}, dimensions={0} | all-to-all | bytes 393216 | tf_op jit(solution)/shard_map/all_to_all | solution.py:387
  104.9 1.0 shard_map.125
  (36 shorter events, 0.2 us)
Async XLA Ops:
  0.6 32.7 %copy-start.6 = (s32[16,1]{0,1:T(1,128)S(1)}, s32[16,1]{0,1:T(1,128)}, u32[]{:S(2)}) copy-start(s32[16,1]{0,1:T(1,128)} %param.20) | copy-start | bytes 196
  0.6 32.9 %copy-start.11 = (s32[16,8]{0,1:T(8,128)S(1)}, s32[16,8]{0,1:T(8,128)}, u32[]{:S(2)}) copy-start(s32[16,8]{0,1:T(8,128)} %param.23) | copy-start | bytes 1540
  0.7 32.9 %copy-start.8 = (s32[16]{0:T(128)S(1)}, s32[16]{0:T(128)}, u32[]{:S(2)}) copy-start(s32[16]{0:T(128)} %tile_ref.1) | copy-start | bytes 196
  0.7 33.8 %copy-start.9 = (bf16[16,3,16,16]{3,2,1,0:T(8,128)(2,1)S(1)}, bf16[16,3,16,16]{3,2,1,0:T(8,128)(2,1)}, u32[]{:S(2)}) copy-start(bf16[16,3,16,16]{3,2,1,0:T(8,128)(2,1)} %param.17) | copy-start | bytes 73732
  25.8 9.6 %copy-start.10 = (bf16[16,3,12,12]{3,0,2,1:T(8,128)(2,1)S(1)}, bf16[16,3,12,12]{3,0,2,1:T(8,128)(2,1)}, u32[]{:S(2)}) copy-start(bf16[16,3,12,12]{3,0,2,1:T(8,128)(2,1)} %param.16) | copy-start | bytes 41476
  25.8 12.1 %copy-start = (bf16[16,3,128,128]{3,2,1,0:T(8,128)(2,1)S(1)}, bf16[16,3,128,128]{3,2,1,0:T(8,128)(2,1)}, u32[]{:S(2)}) copy-start(bf16[16,3,128,128]{3,2,1,0:T(8,128)(2,1)} %z_ref.1) | copy-start | bytes 4718596
  25.8 27.4 %all-to-all-start = ((bf16[16,192,128]{2,1,0:T(8,128)(2,1)}), bf16[16,192,128]{2,1,0:T(8,128)(2,1)}, u32[]{:S(2)}, u32[]{:S(2)}) async-start(bf16[16,192,128]{2,1,0:T(8,128)(2,1)} %shard_map.123), calls=%async_computation | async-start | bytes 1572864 | tf_op jit(solution)/shard_map/all_to_all | solution.py:347
  37.9 0.9 copy-start.12
  37.9 1.0 copy-start.13
  38.8 14.5 %copy-start.1 = (bf16[16,3,128,128]{3,2,1,0:T(8,128)(2,1)S(1)}, bf16[16,3,128,128]{3,2,1,0:T(8,128)(2,1)}, u32[]{:S(2)}) copy-start(bf16[16,3,128,128]{3,2,1,0:T(8,128)(2,1)} %z_ref.1) | copy-start | bytes 4718596
  38.8 14.5 %copy-start.5 = (f32[192,128]{1,0:T(8,128)S(1)}, f32[192,128]{1,0:T(8,128)}, u32[]{:S(2)}) copy-start(f32[192,128]{1,0:T(8,128)} %estimate_ref.1) | copy-start | bytes 294916
  38.8 14.5 %copy-start.7 = (s32[16]{0:T(128)S(1)}, s32[16]{0:T(128)}, u32[]{:S(2)}) copy-start(s32[16]{0:T(128)} %source_ref.3) | copy-start | bytes 196
  53.3 2.1 %copy-start.2 = (bf16[16,192,576]{2,1,0:T(8,128)(2,1)S(1)}, bf16[16,192,576]{2,1,0:T(8,128)(2,1)}, u32[]{:S(2)}) copy-start(bf16[16,192,576]{2,1,0:T(8,128)(2,1)} %get-tuple-element.19.front_hbm) | copy-start | bytes 10616836
  55.4 2.1 %copy-start.3 = (bf16[16,192,576]{2,1,0:T(8,128)(2,1)S(1)}, bf16[16,192,576]{2,1,0:T(8,128)(2,1)}, u32[]{:S(2)}) copy-start(bf16[16,192,576]{2,1,0:T(8,128)(2,1)} %get-tuple-element.20.back_hbm) | copy-start | bytes 10616836
  57.6 1.4 %copy-start.4 = (f32[16,192,128]{2,1,0:T(8,128)S(1)}, f32[16,192,128]{2,1,0:T(8,128)}, u32[]{:S(2)}) copy-start(f32[16,192,128]{2,1,0:T(8,128)} %get-tuple-element.21.log_hbm) | copy-start | bytes 4718596
